TPU v7x, 512 devices: a whole 4x8x8 slice. The times are simulated.
512 devices in a mesh: group: 16 (over y, core), sub: 32 (over z, x).
Axes of the slice: x: 4, y: 8, z: 8, core: 2. Of those that a mesh axis runs over, the one named last changes fastest.
Arguments:
- right_side: float32 [262144, 128], P(('group', 'sub')), may hold values from -6 to 6
- mass: float32 [512, 512], P(('group', 'sub')), may hold values from 0.05 to 0.5
- block_values: float32 [262144, 512], P(('group', 'sub')), may hold values from 0.000390625 to 0.005859375
- block_cols: int32 [4096, 8], P(('group', 'sub')), may hold values from 0 to 7, as said below
- face_rows: int32 [512, 256], P(('group', 'sub')), may hold values from 0 to 511, as said below
- land_rows: int32 [512, 256], P(('group', 'sub')), may hold values from 0 to 511, as said below
- face_counts: int32 [512, 32], P(('group', 'sub')), may hold values from 0 to 8, as said below
- face_weight: float32 [512, 256], P(('group', 'sub')), may hold values from 0.3 to 3
- local_factor: float32 [262144, 128], P(('group', 'sub')), may hold values from -0.25 to 0.25
- basis: float32 [32768, 512], P(('group', 'sub')), may hold values from -0.25 to 0.25
- coarse_inverse: float32 [2048, 2048], P('sub'), may hold values from -1 to 2.5, as said below
Outputs:
- solution_field: float32 [262144, 128], P(('group', 'sub'))
- residual: float32 [262144, 128], P(('group', 'sub'))
Inputs may be any that keep to these rules, and one draw needn't show every extreme that they name: `block_cols`: for each k, the column blocks of a subdomain's 8 block rows are a permutation of 0 to 7. `face_rows`: the 256 entries of a subdomain are distinct local rows. `land_rows`: the 256 entries of a subdomain are distinct local rows. `face_counts`: every subdomain has 8 live slots toward at least one peer. `coarse_inverse`: symmetric positive definite.
All inputs are finite; a program needn't handle non-finite values.
Results may differ from a plain program's by a relative error of at most 0.0003.
Values sent between devices are 32-bit elements; how exact they have to be, the bound alone decides.
No kernel may reach another device: no remote copies, remote signals or barrier semaphores. Data moves between devices by JAX's collectives and lax.ppermute only.
A program may use at most 64 MiB of HBM per device.

v0:
```python
import jax
import jax.numpy as jnp
from jax import lax
from jax.sharding import PartitionSpec as P

ITERS = 3
highest = lax.Precision.HIGHEST


def local(
    right_side,
    mass,
    block_values,
    block_cols,
    face_rows,
    land_rows,
    face_counts,
    face_weight,
    local_factor,
    basis,
    coarse_inverse,
):
    n_rows, n_rhs = right_side.shape
    n_peers = lax.axis_size("sub")
    n_slots = face_rows.shape[1]
    per_peer = n_slots // n_peers
    n_blocks, n_stored = block_cols.shape
    block_rows = n_rows // n_blocks
    n_coarse = basis.shape[0]
    factor_rows = local_factor.shape[1]
    faces = face_rows[0]
    lands = land_rows[0]
    slot_ids = jnp.arange(n_slots)
    live = slot_ids % per_peer < face_counts[0][slot_ids // per_peer]
    weights = jnp.where(live, face_weight[0], jnp.float32(0.0))
    received = lax.all_to_all(weights, "sub", split_axis=0, concat_axis=0, tiled=True)
    values_r = block_values.reshape(n_blocks, block_rows, n_stored * block_rows)
    flat_cols = block_cols.reshape(-1)
    row_total = jnp.sum(block_values, axis=1)
    col_part = jnp.sum(values_r, axis=1).reshape(n_blocks * n_stored, block_rows)
    col_total = (
        jnp.zeros((n_blocks, block_rows), jnp.float32).at[flat_cols].add(col_part).reshape(n_rows)
    )
    degree = (row_total + col_total).at[faces].add(weights).at[lands].add(received)
    diag_col = (mass[0] + degree)[:, None]
    factor_r = local_factor.reshape(n_rows // factor_rows, factor_rows, factor_rows)

    def precondition(resid):
        jacobi = resid / diag_col
        blocks = resid.reshape(n_rows // factor_rows, factor_rows, n_rhs)
        inner = jnp.einsum("bij,bjc->bic", factor_r, blocks, precision=highest)
        local_part = jnp.einsum("bji,bjc->bic", factor_r, inner, precision=highest).reshape(
            n_rows, n_rhs
        )
        coarse_part = jnp.dot(basis, resid, precision=highest)
        total_coarse = coarse_inverse.shape[1]
        start = lax.axis_index("sub") * n_coarse
        padded = lax.dynamic_update_slice_in_dim(
            jnp.zeros((total_coarse, n_rhs), jnp.float32), coarse_part, start, 0
        )
        whole = lax.psum(padded, ("group", "sub"))
        solved = jnp.dot(coarse_inverse, whole, precision=highest)
        coarse_term = jnp.einsum("nr,nc->rc", basis, solved, precision=highest)
        return jacobi + local_part + coarse_term

    def residual_product(resid, zvalue):
        return lax.psum(jnp.sum(resid * zvalue, axis=0), ("group", "sub"))

    resid = right_side
    solution = jnp.zeros_like(right_side)
    zvalue = precondition(resid)
    direction = zvalue
    gamma = residual_product(resid, zvalue)
    for iteration in range(ITERS):
        got_out = lax.all_to_all(
            weights[:, None] * direction[faces], "sub", split_axis=0, concat_axis=0, tiled=True
        )
        got_back = lax.all_to_all(direction[lands], "sub", split_axis=0, concat_axis=0, tiled=True)
        operate_blocks = direction.reshape(n_blocks, block_rows, n_rhs)
        picked = operate_blocks[block_cols].reshape(n_blocks, n_stored * block_rows, n_rhs)
        forward = jnp.einsum("rik,rkc->ric", values_r, picked, precision=highest).reshape(
            n_rows, n_rhs
        )
        back_terms = jnp.einsum(
            "rik,ric->rkc", values_r, operate_blocks, precision=highest
        ).reshape(n_blocks * n_stored, block_rows, n_rhs)
        backward = (
            jnp.zeros((n_blocks, block_rows, n_rhs), jnp.float32)
            .at[flat_cols]
            .add(back_terms)
            .reshape(n_rows, n_rhs)
        )
        coupled = jnp.zeros((n_rows, n_rhs), jnp.float32).at[lands].add(got_out)
        coupled = coupled.at[faces].add(weights[:, None] * got_back)
        image = diag_col * direction - forward - backward - coupled
        alpha = gamma / lax.psum(jnp.sum(direction * image, axis=0), ("group", "sub"))
        solution = solution + alpha * direction
        resid = resid - alpha * image
        if iteration + 1 < ITERS:
            zvalue = precondition(resid)
            gamma_new = residual_product(resid, zvalue)
            direction = zvalue + gamma_new / gamma * direction
            gamma = gamma_new
    return (solution, resid)


def solution(mesh):
    placed = (
        P(("group", "sub"), None),
        P(("group", "sub"), None),
        P(("group", "sub"), None),
        P(("group", "sub"), None),
        P(("group", "sub"), None),
        P(("group", "sub"), None),
        P(("group", "sub"), None),
        P(("group", "sub"), None),
        P(("group", "sub"), None),
        P(("group", "sub"), None),
        P("sub", None),
    )
    return jax.shard_map(
        local,
        mesh=mesh,
        in_specs=placed,
        out_specs=(P(("group", "sub"), None), P(("group", "sub"), None)),
        check_vma=False,
    )
```

profile of v0, /device:TPU:1, one launch (start us, length us, event | category | flops | bytes accessed | tf_op | source)
XLA Modules:
  0.0 1505.4 jit_solution(3155422974275814790)
XLA Ops:
  7.2 2.1 fusion.37
  9.3 1.8 fusion.38
  11.5 5.2 compare_select_fusion.3
  16.7 16.3 %compare_select_fusion.11 = (f32[256]{0:T(256)S(1)}, s32[256]{0:T(256)S(1)}) fusion(f32[256]{0:T(256)} %bitcast.231, pred[256]{0:T(512)(128)(4,1)S(1)} %get-tuple-element.59, pred[256]{0:T(512)(128)(4,1)S(1)} %get-tuple-element.60, pred[256]{0:T(512)(128)(4,1)S(1)} %get-tuple-element.61, pred[256]{0:T(512)(128)(4,1)S(1)} %get-tuple-element.62, ...), kind=kLoop, calls=%fused_computation.136 | loop fusion | flops 8448 | bytes 10596 | tf_op jit(solution)/shard_map/jit(_where)/select_n | solution.py:35
  35.7 13.7 all-to-all-start
  55.7 2.3 scatter_fusion
  58.8 2.3 scatter_fusion.1
  61.1 268.2 %all-reduce.5.cloned.1.call-done = f32[2048,128]{1,0:T(8,128)} async-done(((f32[2048,128]{1,0:T(8,128)}), f32[2048,128]{1,0:T(8,128)}) %all-reduce.5.cloned.1.call-update) | async-done | bytes 1048592 | tf_op jit(solution)/shard_map/psum | solution.py:61
  329.4 2.0 fusion.41
  333.5 6.8 all-to-all-start.1
  340.3 3.2 convolution_bitcast_fusion.2
  343.5 2.9 copy.84
  346.4 7.0 scatter_fusion.2
  353.6 2.0 gather_fusion
  357.1 9.2 all-to-all-start.2
  366.4 3.2 fusion.42
  369.7 1.6 scatter_custom_fusion.4
  371.3 4.4 all-to-all-done.2
  375.7 2.3 scatter_custom_fusion.5
  378.9 97.2 %all-reduce = (f32[128]{0:T(128)S(1)}, f32[128]{0:T(128)S(1)}) all-reduce(f32[128]{0:T(128)} %get-tuple-element.9, f32[128]{0:T(128)} %get-tuple-element.8), channel_id=1, replica_groups=mesh['group'=16,'sub'=32] {'group','sub'}, use_global_device_ids=true, to_apply=%region_7.8 | all-reduce | flops 256 | bytes 2048 | tf_op jit(solution)/shard_map/psum | solution.py:67
  479.7 265.3 %all-reduce.7.cloned.1.call-done = f32[2048,128]{1,0:T(8,128)} async-done(((f32[2048,128]{1,0:T(8,128)}), f32[2048,128]{1,0:T(8,128)}) %all-reduce.7.cloned.1.call-update) | async-done | bytes 1048592 | tf_op jit(solution)/shard_map/psum | solution.py:61
  745.1 2.0 fusion.44
  747.6 97.2 %psum.67 = f32[128]{0:T(128)S(1)} all-reduce(f32[128]{0:T(128)S(1)} %get-tuple-element.53), channel_id=1, replica_groups=mesh['group'=16,'sub'=32] {'group','sub'}, use_global_device_ids=true, to_apply=%region_15.16 | all-reduce | flops 128 | bytes 1024 | tf_op jit(solution)/shard_map/psum | solution.py:67
  847.2 2.0 gather_fusion.3
  850.0 5.9 all-to-all-start.3
  855.9 3.2 convolution_bitcast_fusion.1
  859.1 2.9 copy.95
  862.0 7.0 scatter_fusion.3
  869.2 9.5 all-to-all-start.4
  878.8 3.2 fusion.45
  882.1 1.9 scatter_custom_fusion.7
  883.9 4.1 all-to-all-done.4
  888.0 2.5 scatter_custom_fusion.8
  891.3 95.4 %psum.68 = f32[128]{0:T(128)S(1)} all-reduce(f32[128]{0:T(128)} %get-tuple-element.14), channel_id=1, replica_groups=mesh['group'=16,'sub'=32] {'group','sub'}, use_global_device_ids=true, to_apply=%region_20.21 | all-reduce | flops 128 | bytes 1024 | tf_op jit(solution)/shard_map/psum | solution.py:96
  990.9 265.1 %all-reduce.9.cloned.1.call-done = f32[2048,128]{1,0:T(8,128)} async-done(((f32[2048,128]{1,0:T(8,128)}), f32[2048,128]{1,0:T(8,128)}) %all-reduce.9.cloned.1.call-update) | async-done | bytes 1048592 | tf_op jit(solution)/shard_map/psum | solution.py:61
  1256.1 2.0 fusion.47
  1258.6 97.4 %psum.70 = f32[128]{0:T(128)S(1)} all-reduce(f32[128]{0:T(128)S(1)} %get-tuple-element.55), channel_id=1, replica_groups=mesh['group'=16,'sub'=32] {'group','sub'}, use_global_device_ids=true, to_apply=%region_23.24 | all-reduce | flops 128 | bytes 1024 | tf_op jit(solution)/shard_map/psum | solution.py:67
  1358.4 2.0 gather_fusion.6
  1361.2 5.7 all-to-all-start.5
  1366.9 3.2 convolution_bitcast_fusion
  1370.1 2.9 copy.105
  1373.0 7.0 scatter_fusion.4
  1380.2 9.2 all-to-all-start.6
  1389.5 3.2 fusion.48
  1392.8 1.6 scatter_custom_fusion.10
  1394.4 4.4 all-to-all-done.6
  1398.8 2.3 scatter_custom_fusion.11
  1401.4 95.4 %psum.71 = f32[128]{0:T(128)S(1)} all-reduce(f32[128]{0:T(128)S(1)} %get-tuple-element.12), channel_id=1, replica_groups=mesh['group'=16,'sub'=32] {'group','sub'}, use_global_device_ids=true, to_apply=%region_28.29 | all-reduce | flops 128 | bytes 1024 | tf_op jit(solution)/shard_map/psum | solution.py:96
  (167 shorter events, 33.3 us)
Async XLA Ops:
  7.2 322.2 %copy-start = (f32[64,2048]{1,0:T(8,128)S(1)}, f32[64,2048]{1,0:T(8,128)}, u32[]{:S(2)}) copy-start(f32[64,2048]{1,0:T(8,128)} %param.21) | copy-start | bytes 1572868
  7.2 45.0 %copy-start.17 = (f32[1,256]{1,0:T(1,128)S(1)}, f32[1,256]{1,0:T(1,128)}, u32[]{:S(2)}) copy-start(f32[1,256]{1,0:T(1,128)} %param.18) | copy-start | bytes 3076
  7.2 44.8 %copy-start.14 = (s32[8,8]{1,0:T(8,128)S(1)}, s32[8,8]{1,0:T(8,128)}, u32[]{:S(2)}) copy-start(s32[8,8]{1,0:T(8,128)} %param.14) | copy-start | bytes 772
  7.2 45.0 %copy-start.1 = (f32[512,512]{1,0:T(8,128)S(1)}, f32[512,512]{1,0:T(8,128)}, u32[]{:S(2)}) copy-start(f32[512,512]{1,0:T(8,128)} %param.13) | copy-start | bytes 3145732
  16.7 39.0 %copy-start.16 = (s32[256,1]{0,1:T(1,128)}, s32[256,1]{0,1:T(1,128)S(1)}, u32[]{:S(2)}) copy-start(s32[256,1]{0,1:T(1,128)S(1)} %get-tuple-element.57) | copy-start | bytes 3076
  35.7 22.3 %all-to-all-start = ((f32[32,8,1]{1,2,0:T(1,128)}), f32[32,8,1]{1,2,0:T(1,128)S(1)}, u32[]{:S(2)}, u32[]{:S(2)}) async-start(f32[32,8,1]{1,2,0:T(1,128)} %bitcast.41), calls=%async_computation | async-start | bytes 32768 | tf_op jit(solution)/shard_map/all_to_all | solution.py:36
  49.4 280.0 %all-reduce.5.cloned.1.call-start = ((), (), s32[]{:S(2)}) async-start(), calls=%async_computation.7 | async-start | bytes 2097152 | tf_op jit(solution)/shard_map/psum | solution.py:61
  49.5 4.1 copy-start.26
  49.5 4.2 copy-start.2
  49.5 4.2 copy-start.8
  50.9 1.0 copy-start.4
  50.9 3.2 copy-start.21
  52.3 294.1 %copy-start.18 = (s32[64]{0:T(128)}, s32[64]{0:T(128)S(1)}, u32[]{:S(2)}) copy-start(s32[64]{0:T(128)S(1)} %fusion.36) | copy-start | bytes 772
  53.6 5.2 copy-start.15
  54.1 278.6 %copy-start.11 = (f32[32,8]{1,0:T(8,128)}, f32[32,8]{1,0:T(8,128)S(1)}, u32[]{:S(2)}) copy-start(f32[32,8]{1,0:T(8,128)S(1)} %fusion.32) | copy-start | bytes 3076
  58.0 273.4 %copy-start.9 = (f32[64,512]{1,0:T(8,128)S(1)}, f32[64,512]{1,0:T(8,128)}, u32[]{:S(2)}) copy-start(f32[64,512]{1,0:T(8,128)} %param.20) | copy-start | bytes 393220
  331.8 512.9 %copy-start.6 = (f32[512,128]{0,1:T(8,128)}, f32[512,128]{0,1:T(8,128)S(1)}, u32[]{:S(2)}) copy-start(f32[512,128]{0,1:T(8,128)S(1)} %fusion.2) | copy-start | bytes 786436
  333.5 23.6 %all-to-all-start.1 = ((f32[32,8,128]{2,1,0:T(8,128)}), f32[32,8,128]{2,1,0:T(8,128)S(1)}, u32[]{:S(2)}, u32[]{:S(2)}) async-start(f32[32,8,128]{2,1,0:T(8,128)} %bitcast_multiply_fusion.8), calls=%async_computation.1 | async-start | bytes 262144 | tf_op jit(solution)/shard_map/all_to_all | solution.py:75
  357.1 18.6 %all-to-all-start.2 = ((f32[32,8,128]{2,1,0:T(8,128)}), f32[32,8,128]{2,1,0:T(8,128)S(1)}, u32[]{:S(2)}, u32[]{:S(2)}) async-start(f32[32,8,128]{2,1,0:T(8,128)} %bitcast.56), calls=%async_computation.2 | async-start | bytes 262144 | tf_op jit(solution)/shard_map/all_to_all | solution.py:78
  366.3 378.7 %all-reduce.7.cloned.1.call-start = ((), (), s32[]{:S(2)}) async-start(), calls=%async_computation.8 | async-start | bytes 2097152 | tf_op jit(solution)/shard_map/psum | solution.py:61
  476.1 0.5 copy-start.29
  476.1 0.6 copy-start.22
  477.2 1.0 copy-start.5
  479.0 365.8 %copy-start.30 = (f32[128]{0:T(128)S(1)}, f32[128]{0:T(128)}, u32[]{:S(2)}) copy-start(f32[128]{0:T(128)} %copy-done.29) | copy-start | bytes 1540
  844.8 4.5 copy-start.27
  847.2 2.0 copy-start.12
  850.0 19.2 %all-to-all-start.3 = ((f32[32,8,128]{2,1,0:T(8,128)}), f32[32,8,128]{2,1,0:T(8,128)S(1)}, u32[]{:S(2)}, u32[]{:S(2)}) async-start(f32[32,8,128]{2,1,0:T(8,128)} %bitcast_multiply_fusion.5), calls=%async_computation.3 | async-start | bytes 262144 | tf_op jit(solution)/shard_map/all_to_all | solution.py:75
  859.1 2.9 copy-start.19
  869.2 9.6 copy-start.10
  869.2 18.8 %all-to-all-start.4 = ((f32[32,8,128]{2,1,0:T(8,128)}), f32[32,8,128]{2,1,0:T(8,128)}, u32[]{:S(2)}, u32[]{:S(2)}) async-start(f32[32,8,128]{2,1,0:T(8,128)} %bitcast.71), calls=%async_computation.4 | async-start | bytes 262144 | tf_op jit(solution)/shard_map/all_to_all | solution.py:78
  878.7 377.4 %all-reduce.9.cloned.1.call-start = ((), (), s32[]{:S(2)}) async-start(), calls=%async_computation.9 | async-start | bytes 2097152 | tf_op jit(solution)/shard_map/psum | solution.py:61
  987.3 0.6 copy-start.24
  988.5 1.0 copy-start.3
  990.2 365.8 %copy-start.28 = (f32[128]{0:T(128)S(1)}, f32[128]{0:T(128)}, u32[]{:S(2)}) copy-start(f32[128]{0:T(128)} %copy-done.27) | copy-start | bytes 1540
  1358.4 2.0 copy-start.13
  1361.2 19.0 %all-to-all-start.5 = ((f32[32,8,128]{2,1,0:T(8,128)}), f32[32,8,128]{2,1,0:T(8,128)S(1)}, u32[]{:S(2)}, u32[]{:S(2)}) async-start(f32[32,8,128]{2,1,0:T(8,128)} %bitcast_multiply_fusion.2), calls=%async_computation.5 | async-start | bytes 262144 | tf_op jit(solution)/shard_map/all_to_all | solution.py:75
  1370.1 2.9 copy-start.20
  1380.2 18.6 %all-to-all-start.6 = ((f32[32,8,128]{2,1,0:T(8,128)}), f32[32,8,128]{2,1,0:T(8,128)S(1)}, u32[]{:S(2)}, u32[]{:S(2)}) async-start(f32[32,8,128]{2,1,0:T(8,128)} %bitcast.86), calls=%async_computation.6 | async-start | bytes 262144 | tf_op jit(solution)/shard_map/all_to_all | solution.py:78
  1392.6 104.2 %copy-start.7 = (f32[512,128]{0,1:T(8,128)S(1)}, f32[512,128]{0,1:T(8,128)}, u32[]{:S(2)}) copy-start(f32[512,128]{0,1:T(8,128)} %copy-done.6) | copy-start | bytes 786436
  1392.6 104.2 %copy-start.23 = (f32[128]{0:T(128)S(1)}, f32[128]{0:T(128)}, u32[]{:S(2)}) copy-start(f32[128]{0:T(128)} %copy-done.22) | copy-start | bytes 1540
  1392.7 104.2 %copy-start.25 = (f32[128]{0:T(128)S(1)}, f32[128]{0:T(128)}, u32[]{:S(2)}) copy-start(f32[128]{0:T(128)} %copy-done.24) | copy-start | bytes 1540
Sparse Core Ops, SparseCore 0:
  55.3 274.0 all-reduce.4
  478.4 266.6 all-reduce.6
  989.7 266.3 all-reduce.8
where the time goes:
time: 1520 us; the launch traced here: 1510 us
  waiting for transfers between devices  812 us (53%)
  blocking collectives  483 us (32%)
  other arithmetic  69.2 us (5%)
  starting transfers between devices  60.2 us (4%)
  local copies, waits for them, and re-layouts  34.9 us (2%)
  matrix products  32.1 us (2%)
    psum x3, waiting for transfers between devices, precondition(): whole = lax.psum(padded, ('group', 'sub'))  799 us
    psum x3, blocking collectives, residual_product(): return lax.psum(jnp.sum(resid * zvalue, axis=0), ('group', 'sub'))  292 us
    psum x2, blocking collectives, local(): lax.psum(jnp.sum(direction * image, axis=0), ('group', 'sub'))  191 us
  transfers between devices with their start and end apart: 10, of which 6 were waited for; matrix products, arithmetic and copies ran while one was open for 5% of the time, Pallas kernels for 0%

commit v1 on v0

--- a/solution.py
+++ b/solution.py
@@ -5,6 +5,10 @@
 
 ITERS = 3
 highest = lax.Precision.HIGHEST
+
+
+def put_routes_all_up(array_here):
+    return lax.psum(lax.psum(array_here, "sub"), axis_name="group")
 
 
 def local(
@@ -64,7 +68,7 @@
         return jacobi + local_part + coarse_term
 
     def residual_product(resid, zvalue):
-        return lax.psum(jnp.sum(resid * zvalue, axis=0), ("group", "sub"))
+        return put_routes_all_up(jnp.sum(resid * zvalue, axis=0))
 
     resid = right_side
     solution = jnp.zeros_like(right_side)

time: 1520 us -> 1610 us (1.059)
  blocking collectives: 483 us -> 572 us
    psum x2 -> x3, blocking collectives: 191 us -> 284 us  [local(): lax.psum(jnp.sum(direction * image, axis=0), ('group', 'sub'))]
    psum x3 -> x6, blocking collectives: 292 us -> 288 us  [put_routes_all_up(): return lax.psum(lax.psum(array_here, 'sub'), axis_name='group')]
  transfers between devices with their start and end apart: 10 -> 10, of which waited for: 6 -> 6; matrix products, arithmetic and copies ran while one was open for 5% -> 4% of each run, Pallas kernels for 0% -> 0%
where the time goes in v1:
time: 1610 us; the launch traced here: 1600 us
  waiting for transfers between devices  813 us (50%)
  blocking collectives  572 us (36%)
  other arithmetic  69.2 us (4%)
  starting transfers between devices  63.1 us (4%)
  local copies, waits for them, and re-layouts  34.9 us (2%)
  matrix products  32.1 us (2%)
    psum x3, waiting for transfers between devices, precondition(): whole = lax.psum(padded, ('group', 'sub'))  800 us
    psum x6, blocking collectives, put_routes_all_up(): return lax.psum(lax.psum(array_here, 'sub'), axis_name='group')  288 us
    psum x3, blocking collectives, local(): lax.psum(jnp.sum(direction * image, axis=0), ('group', 'sub'))  284 us
  transfers between devices with their start and end apart: 10, of which 6 were waited for; matrix products, arithmetic and copies ran while one was open for 4% of the time, Pallas kernels for 0%

profile of v1, /device:TPU:1, one launch (start us, length us, event | category | flops | bytes accessed | tf_op | source)
XLA Modules:
  0.0 1599.3 jit_solution(906750239872124390)
XLA Ops:
  7.2 2.1 fusion.37
  11.5 5.2 compare_select_fusion.3
  16.7 16.3 %compare_select_fusion.11 = (f32[256]{0:T(256)S(1)}, s32[256]{0:T(256)S(1)}) fusion(f32[256]{0:T(256)} %bitcast.231, pred[256]{0:T(512)(128)(4,1)S(1)} %get-tuple-element.57, pred[256]{0:T(512)(128)(4,1)S(1)} %get-tuple-element.58, pred[256]{0:T(512)(128)(4,1)S(1)} %get-tuple-element.59, pred[256]{0:T(512)(128)(4,1)S(1)} %get-tuple-element.60, ...), kind=kLoop, calls=%fused_computation.136 | loop fusion | flops 8448 | bytes 10596 | tf_op jit(solution)/shard_map/jit(_where)/select_n | solution.py:39
  35.7 13.7 all-to-all-start
  55.7 2.3 scatter_fusion
  58.8 2.3 scatter_fusion.1
  61.1 268.2 %all-reduce.4.cloned.1.call-done = f32[2048,128]{1,0:T(8,128)} async-done(((f32[2048,128]{1,0:T(8,128)}), f32[2048,128]{1,0:T(8,128)}) %all-reduce.4.cloned.1.call-update) | async-done | bytes 1048592 | tf_op jit(solution)/shard_map/psum | solution.py:65
  329.4 2.0 fusion.41
  333.5 6.8 all-to-all-start.1
  340.3 3.2 convolution_bitcast_fusion.2
  343.5 2.9 copy.84
  346.4 7.0 scatter_fusion.2
  353.6 2.0 gather_fusion
  357.1 9.2 all-to-all-start.2
  366.4 3.2 fusion.42
  371.3 4.4 all-to-all-done.2
  375.7 2.3 scatter_custom_fusion.5
  378.9 56.8 %psum.85 = f32[128]{0:T(128)S(1)} all-reduce(f32[128]{0:T(128)} %get-tuple-element.9), channel_id=1, replica_groups=mesh['group'=16,'sub'=32] {'sub'}, use_global_device_ids=true, to_apply=%region_7.8 | all-reduce | flops 128 | bytes 1024 | tf_op jit(solution)/shard_map/psum | solution.py:11
  435.7 40.3 %psum.86 = f32[128]{0:T(128)S(1)} all-reduce(f32[128]{0:T(128)S(1)} %psum.85), channel_id=1, replica_groups=mesh['group'=16,'sub'=32] {'group'}, use_global_device_ids=true, to_apply=%region_8.9 | all-reduce | flops 128 | bytes 1024 | tf_op jit(solution)/shard_map/psum | solution.py:11
  476.0 93.6 %psum.87 = f32[128]{0:T(128)S(1)} all-reduce(f32[128]{0:T(128)} %get-tuple-element.8), channel_id=1, replica_groups=mesh['group'=16,'sub'=32] {'group','sub'}, use_global_device_ids=true, to_apply=%region_13.14 | all-reduce | flops 128 | bytes 1024 | tf_op jit(solution)/shard_map/psum | solution.py:100
  573.2 266.1 %all-reduce.6.cloned.1.call-done = f32[2048,128]{1,0:T(8,128)} async-done(((f32[2048,128]{1,0:T(8,128)}), f32[2048,128]{1,0:T(8,128)}) %all-reduce.6.cloned.1.call-update) | async-done | bytes 1048592 | tf_op jit(solution)/shard_map/psum | solution.py:65
  839.3 2.0 fusion.44
  841.8 58.4 %psum.89 = f32[128]{0:T(128)S(1)} all-reduce(f32[128]{0:T(128)S(1)} %get-tuple-element.51), channel_id=1, replica_groups=mesh['group'=16,'sub'=32] {'sub'}, use_global_device_ids=true, to_apply=%region_16.17 | all-reduce | flops 128 | bytes 1024 | tf_op jit(solution)/shard_map/psum | solution.py:11
  900.2 37.0 %psum.90 = f32[128]{0:T(128)S(1)} all-reduce(f32[128]{0:T(128)S(1)} %psum.89), channel_id=1, replica_groups=mesh['group'=16,'sub'=32] {'group'}, use_global_device_ids=true, to_apply=%region_17.18 | all-reduce | flops 128 | bytes 1024 | tf_op jit(solution)/shard_map/psum | solution.py:11
  939.7 2.0 gather_fusion.3
  942.5 7.4 all-to-all-start.3
  949.8 3.2 convolution_bitcast_fusion.1
  953.0 2.9 copy.95
  955.9 7.0 scatter_fusion.3
  963.1 9.5 all-to-all-start.4
  972.7 3.2 fusion.45
  977.8 4.1 all-to-all-done.4
  981.9 2.5 scatter_custom_fusion.8
  985.2 95.1 %psum.91 = f32[128]{0:T(128)S(1)} all-reduce(f32[128]{0:T(128)} %get-tuple-element.12), channel_id=1, replica_groups=mesh['group'=16,'sub'=32] {'group','sub'}, use_global_device_ids=true, to_apply=%region_22.23 | all-reduce | flops 128 | bytes 1024 | tf_op jit(solution)/shard_map/psum | solution.py:100
  1084.6 266.1 %all-reduce.8.cloned.1.call-done = f32[2048,128]{1,0:T(8,128)} async-done(((f32[2048,128]{1,0:T(8,128)}), f32[2048,128]{1,0:T(8,128)}) %all-reduce.8.cloned.1.call-update) | async-done | bytes 1048592 | tf_op jit(solution)/shard_map/psum | solution.py:65
  1350.7 2.0 fusion.47
  1353.2 58.4 %psum.93 = f32[128]{0:T(128)S(1)} all-reduce(f32[128]{0:T(128)S(1)} %get-tuple-element.53), channel_id=1, replica_groups=mesh['group'=16,'sub'=32] {'sub'}, use_global_device_ids=true, to_apply=%region_25.26 | all-reduce | flops 128 | bytes 1024 | tf_op jit(solution)/shard_map/psum | solution.py:11
  1411.7 37.0 %psum.94 = f32[128]{0:T(128)S(1)} all-reduce(f32[128]{0:T(128)S(1)} %psum.93), channel_id=1, replica_groups=mesh['group'=16,'sub'=32] {'group'}, use_global_device_ids=true, to_apply=%region_26.27 | all-reduce | flops 128 | bytes 1024 | tf_op jit(solution)/shard_map/psum | solution.py:11
  1451.1 2.0 gather_fusion.6
  1453.9 7.2 all-to-all-start.5
  1461.1 3.2 convolution_bitcast_fusion
  1464.3 2.9 copy.105
  1467.2 7.0 scatter_fusion.4
  1474.4 9.2 all-to-all-start.6
  1483.6 3.2 fusion.48
  1488.6 4.4 all-to-all-done.6
  1493.0 2.3 scatter_custom_fusion.11
  1495.5 95.1 %psum.95 = f32[128]{0:T(128)S(1)} all-reduce(f32[128]{0:T(128)S(1)} %get-tuple-element.10), channel_id=1, replica_groups=mesh['group'=16,'sub'=32] {'group','sub'}, use_global_device_ids=true, to_apply=%region_31.32 | all-reduce | flops 128 | bytes 1024 | tf_op jit(solution)/shard_map/psum | solution.py:100
  (171 shorter events, 40.3 us)
Async XLA Ops:
  7.2 322.2 %copy-start = (f32[64,2048]{1,0:T(8,128)S(1)}, f32[64,2048]{1,0:T(8,128)}, u32[]{:S(2)}) copy-start(f32[64,2048]{1,0:T(8,128)} %param.21) | copy-start | bytes 1572868
  7.2 45.0 %copy-start.17 = (f32[1,256]{1,0:T(1,128)S(1)}, f32[1,256]{1,0:T(1,128)}, u32[]{:S(2)}) copy-start(f32[1,256]{1,0:T(1,128)} %param.18) | copy-start | bytes 3076
  7.2 44.8 %copy-start.14 = (s32[8,8]{1,0:T(8,128)S(1)}, s32[8,8]{1,0:T(8,128)}, u32[]{:S(2)}) copy-start(s32[8,8]{1,0:T(8,128)} %param.14) | copy-start | bytes 772
  7.2 45.0 %copy-start.1 = (f32[512,512]{1,0:T(8,128)S(1)}, f32[512,512]{1,0:T(8,128)}, u32[]{:S(2)}) copy-start(f32[512,512]{1,0:T(8,128)} %param.13) | copy-start | bytes 3145732
  16.7 39.0 %copy-start.16 = (s32[256,1]{0,1:T(1,128)}, s32[256,1]{0,1:T(1,128)S(1)}, u32[]{:S(2)}) copy-start(s32[256,1]{0,1:T(1,128)S(1)} %get-tuple-element.55) | copy-start | bytes 3076
  35.7 22.3 %all-to-all-start = ((f32[32,8,1]{1,2,0:T(1,128)}), f32[32,8,1]{1,2,0:T(1,128)S(1)}, u32[]{:S(2)}, u32[]{:S(2)}) async-start(f32[32,8,1]{1,2,0:T(1,128)} %bitcast.41), calls=%async_computation | async-start | bytes 32768 | tf_op jit(solution)/shard_map/all_to_all | solution.py:40
  49.4 280.0 %all-reduce.4.cloned.1.call-start = ((), (), s32[]{:S(2)}) async-start(), calls=%async_computation.7 | async-start | bytes 2097152 | tf_op jit(solution)/shard_map/psum | solution.py:65
  49.5 4.1 copy-start.26
  49.5 4.2 copy-start.2
  49.5 4.2 copy-start.8
  50.9 1.0 copy-start.4
  50.9 3.2 copy-start.21
  52.3 294.1 %copy-start.18 = (s32[64]{0:T(128)}, s32[64]{0:T(128)S(1)}, u32[]{:S(2)}) copy-start(s32[64]{0:T(128)S(1)} %fusion.36) | copy-start | bytes 772
  53.6 5.2 copy-start.15
  54.1 278.6 %copy-start.11 = (f32[32,8]{1,0:T(8,128)}, f32[32,8]{1,0:T(8,128)S(1)}, u32[]{:S(2)}) copy-start(f32[32,8]{1,0:T(8,128)S(1)} %fusion.32) | copy-start | bytes 3076
  58.0 273.4 %copy-start.9 = (f32[64,512]{1,0:T(8,128)S(1)}, f32[64,512]{1,0:T(8,128)}, u32[]{:S(2)}) copy-start(f32[64,512]{1,0:T(8,128)} %param.20) | copy-start | bytes 393220
  331.8 605.4 %copy-start.6 = (f32[512,128]{0,1:T(8,128)}, f32[512,128]{0,1:T(8,128)S(1)}, u32[]{:S(2)}) copy-start(f32[512,128]{0,1:T(8,128)S(1)} %fusion.2) | copy-start | bytes 786436
  333.5 23.6 %all-to-all-start.1 = ((f32[32,8,128]{2,1,0:T(8,128)}), f32[32,8,128]{2,1,0:T(8,128)S(1)}, u32[]{:S(2)}, u32[]{:S(2)}) async-start(f32[32,8,128]{2,1,0:T(8,128)} %bitcast_multiply_fusion.8), calls=%async_computation.1 | async-start | bytes 262144 | tf_op jit(solution)/shard_map/all_to_all | solution.py:79
  357.1 18.6 %all-to-all-start.2 = ((f32[32,8,128]{2,1,0:T(8,128)}), f32[32,8,128]{2,1,0:T(8,128)S(1)}, u32[]{:S(2)}, u32[]{:S(2)}) async-start(f32[32,8,128]{2,1,0:T(8,128)} %bitcast.56), calls=%async_computation.2 | async-start | bytes 262144 | tf_op jit(solution)/shard_map/all_to_all | solution.py:82
  366.3 473.0 %all-reduce.6.cloned.1.call-start = ((), (), s32[]{:S(2)}) async-start(), calls=%async_computation.8 | async-start | bytes 2097152 | tf_op jit(solution)/shard_map/psum | solution.py:65
  476.0 93.6 %copy-start.29 = (f32[128]{0:T(128)}, f32[128]{0:T(128)S(1)}, u32[]{:S(2)}) copy-start(f32[128]{0:T(128)S(1)} %psum.86) | copy-start | bytes 1540
  569.6 0.6 copy-start.22
  570.7 1.0 copy-start.5
  572.4 364.8 %copy-start.30 = (f32[128]{0:T(128)S(1)}, f32[128]{0:T(128)}, u32[]{:S(2)}) copy-start(f32[128]{0:T(128)} %copy-done.29) | copy-start | bytes 1540
  937.2 4.5 copy-start.27
  939.7 2.0 copy-start.12
  942.5 20.7 %all-to-all-start.3 = ((f32[32,8,128]{2,1,0:T(8,128)}), f32[32,8,128]{2,1,0:T(8,128)S(1)}, u32[]{:S(2)}, u32[]{:S(2)}) async-start(f32[32,8,128]{2,1,0:T(8,128)} %bitcast_multiply_fusion.5), calls=%async_computation.3 | async-start | bytes 262144 | tf_op jit(solution)/shard_map/all_to_all | solution.py:79
  953.0 2.9 copy-start.19
  963.1 9.5 copy-start.10
  963.1 18.8 %all-to-all-start.4 = ((f32[32,8,128]{2,1,0:T(8,128)}), f32[32,8,128]{2,1,0:T(8,128)}, u32[]{:S(2)}, u32[]{:S(2)}) async-start(f32[32,8,128]{2,1,0:T(8,128)} %bitcast.71), calls=%async_computation.4 | async-start | bytes 262144 | tf_op jit(solution)/shard_map/all_to_all | solution.py:82
  972.6 378.1 %all-reduce.8.cloned.1.call-start = ((), (), s32[]{:S(2)}) async-start(), calls=%async_computation.9 | async-start | bytes 2097152 | tf_op jit(solution)/shard_map/psum | solution.py:65
  1081.0 0.6 copy-start.24
  1082.1 1.0 copy-start.3
  1083.9 364.8 %copy-start.28 = (f32[128]{0:T(128)S(1)}, f32[128]{0:T(128)}, u32[]{:S(2)}) copy-start(f32[128]{0:T(128)} %copy-done.27) | copy-start | bytes 1540
  1451.1 2.0 copy-start.13
  1453.9 20.5 %all-to-all-start.5 = ((f32[32,8,128]{2,1,0:T(8,128)}), f32[32,8,128]{2,1,0:T(8,128)S(1)}, u32[]{:S(2)}, u32[]{:S(2)}) async-start(f32[32,8,128]{2,1,0:T(8,128)} %bitcast_multiply_fusion.2), calls=%async_computation.5 | async-start | bytes 262144 | tf_op jit(solution)/shard_map/all_to_all | solution.py:79
  1464.3 2.9 copy-start.20
  1474.4 18.6 %all-to-all-start.6 = ((f32[32,8,128]{2,1,0:T(8,128)}), f32[32,8,128]{2,1,0:T(8,128)S(1)}, u32[]{:S(2)}, u32[]{:S(2)}) async-start(f32[32,8,128]{2,1,0:T(8,128)} %bitcast.86), calls=%async_computation.6 | async-start | bytes 262144 | tf_op jit(solution)/shard_map/all_to_all | solution.py:82
  1486.8 103.9 %copy-start.7 = (f32[512,128]{0,1:T(8,128)S(1)}, f32[512,128]{0,1:T(8,128)}, u32[]{:S(2)}) copy-start(f32[512,128]{0,1:T(8,128)} %copy-done.6) | copy-start | bytes 786436
  1486.8 103.9 %copy-start.23 = (f32[128]{0:T(128)S(1)}, f32[128]{0:T(128)}, u32[]{:S(2)}) copy-start(f32[128]{0:T(128)} %copy-done.22) | copy-start | bytes 1540
  1486.8 103.9 %copy-start.25 = (f32[128]{0:T(128)S(1)}, f32[128]{0:T(128)}, u32[]{:S(2)}) copy-start(f32[128]{0:T(128)} %copy-done.24) | copy-start | bytes 1540
Sparse Core Ops, SparseCore 0:
  55.3 274.0 all-reduce.3
  571.9 267.3 all-reduce.5
  1083.3 267.3 all-reduce.7
